TPU v7x, 768 devices: a whole 4x8x12 slice. The times are simulated.
768 devices in a mesh: gx: 24 (over x, z_lo), gy: 32 (over z_hi, y, core).
Axes of the slice: x: 4, y: 8, z: 12 (z_hi: 2, z_lo: 6; z = z_hi * 6 + z_lo), core: 2. Of those that a mesh axis runs over, the one named last changes fastest.
Arguments:
- inputs: bfloat16 [768, 12288], P('gx', 'gy'), may hold values from -6 to 6
- preact: bfloat16 [768, 24576], P('gy', 'gx'), may hold values from -6 to 6
- w_in: bfloat16 [12288, 24576], P('gy', 'gx'), may hold values from -0.0546875 to 0.0546875
- w_out: bfloat16 [24576, 12288], P('gx', 'gy'), may hold values from -0.0390625 to 0.0390625
- out_grad: bfloat16 [768, 12288], P('gx', 'gy'), may hold values from -6 to 6
Outputs:
- grad_inputs: bfloat16 [768, 12288], P('gx', 'gy')
- grad_w_in: bfloat16 [12288, 24576], P('gy', 'gx')
- grad_w_out: bfloat16 [24576, 12288], P('gx', 'gy')
All inputs are finite; a program needn't handle non-finite values.
Results may differ from a plain program's by a relative error of at most 0.0049.
Values may be sent and summed in bfloat16 or wider, within the bound.
A program may use at most 32 MiB of HBM per device.

v0:
```python
import jax
import jax.numpy as jnp
from jax import lax
from jax.sharding import PartitionSpec as P

gelu_scale = 0.7978845608028654
cubic_coef = 0.044715


def activation_pair(grad_act, preact):
    values = preact.astype(jnp.float32)
    argument = gelu_scale * (values + cubic_coef * values * values * values)
    tangent = jnp.tanh(argument)
    acts = (0.5 * values * (1.0 + tangent)).astype(jnp.bfloat16)
    slope = 0.5 * (1.0 + tangent) + 0.5 * values * (1.0 - tangent * tangent) * gelu_scale * (
        1.0 + 3.0 * cubic_coef * values * values
    )
    return (acts, (grad_act * slope).astype(jnp.bfloat16))


def per_device(inputs, preact, w_in, w_out, out_grad):
    input_rows, grad_rows = (
        lax.all_gather(inputs, "gx", axis=0, tiled=True),
        lax.all_gather(out_grad, "gx", axis=0, tiled=True),
    )
    portion = grad_rows
    hidden_rows = lax.psum_scatter(
        lax.dot_general(
            portion, w_out, (((1,), (1,)), ((), ())), preferred_element_type=jnp.float32
        ),
        "gy",
        scatter_dimension=0,
        tiled=True,
    )
    act_rows, hidden_grad_rows = activation_pair(hidden_rows, preact)
    acts, grad_hidden = (
        lax.all_gather(act_rows, "gy", axis=0, tiled=True),
        lax.all_gather(hidden_grad_rows, "gy", axis=0, tiled=True),
    )
    grad_w_out = lax.dot_general(
        acts, grad_rows, (((0,), (0,)), ((), ())), preferred_element_type=jnp.float32
    ).astype(jnp.bfloat16)
    grad_w_in = lax.dot_general(
        input_rows, grad_hidden, (((0,), (0,)), ((), ())), preferred_element_type=jnp.float32
    ).astype(jnp.bfloat16)
    portion = grad_hidden
    grad_inputs = lax.psum_scatter(
        lax.dot_general(
            portion, w_in, (((1,), (1,)), ((), ())), preferred_element_type=jnp.float32
        ),
        "gx",
        scatter_dimension=0,
        tiled=True,
    ).astype(jnp.bfloat16)
    return (grad_inputs, grad_w_in, grad_w_out)


def solution(mesh):
    placed = (P("gx", "gy"), P("gy", "gx"), P("gy", "gx"), P("gx", "gy"), P("gx", "gy"))
    return jax.shard_map(
        per_device,
        mesh=mesh,
        in_specs=placed,
        out_specs=(P("gx", "gy"), P("gy", "gx"), P("gx", "gy")),
        check_vma=False,
    )
```

profile of v0, /device:TPU:8, one launch (start us, length us, event | category | flops | bytes accessed | tf_op | source)
XLA Modules:
  0.0 632.6 jit_solution(2111492468237795311)
XLA Ops:
  7.2 0.0 copy-start
  7.2 0.0 reduce-scatter.3.cloned.1.call-start
  7.2 91.3 %all_gather.12 = bf16[768,384]{1,0:T(8,128)(2,1)S(1)} all-gather(bf16[32,384]{1,0:T(8,128)(2,1)} %param.9), channel_id=1, replica_groups=mesh['gx'=24,'gy'=32] {'gx'}, dimensions={0}, use_global_device_ids=true | all-gather | bytes 614400 | tf_op jit(solution)/shard_map/all_gather | solution.py:24
  98.5 0.0 copy-done
  98.5 2.6 fusion.12
  101.2 0.0 copy-start.1
  101.2 0.0 copy-start.3
  101.2 0.0 reduce-scatter.3.cloned.1.call-update
  101.2 0.0 all-gather.3.cloned.1.call-start
  101.2 161.5 %reduce-scatter.3.cloned.1.call-done = f32[24,1024]{1,0:T(8,128)} async-done(((f32[768,1024]{1,0:T(8,128)}), f32[24,1024]{1,0:T(8,128)}) %reduce-scatter.3.cloned.1.call-update) | async-done | bytes 98320 | tf_op jit(solution)/shard_map/reduce_scatter | solution.py:27
  262.7 0.0 copy-done.1
  262.7 1.6 fusion.8
  264.3 0.0 all-gather.3.cloned.1.call-update
  264.3 0.0 all-gather.5.cloned.1.call-start
  264.4 0.7 all-gather.5.cloned.1.call-update
  265.1 0.0 copy-start.2
  265.1 0.0 reduce-scatter.5.cloned.1.call-start
  265.1 98.0 %all-gather.3.cloned.1.call-done = bf16[768,1024]{1,0:T(8,128)(2,1)} async-done(((bf16[24,1024]{1,0:T(8,128)(2,1)}), bf16[768,1024]{1,0:T(8,128)(2,1)}) %all-gather.3.cloned.1.call-update) | async-done | bytes 1572880 | tf_op jit(solution)/shard_map/all_gather | solution.py:38
  363.1 0.0 copy-done.3
  363.1 3.4 fusion.13
  366.6 0.0 reduce-scatter.5.cloned.1.call-update
  366.6 0.0 copy-done.2
  366.6 87.3 %all_gather.14 = bf16[768,384]{1,0:T(8,128)(2,1)S(1)} all-gather(bf16[32,384]{1,0:T(8,128)(2,1)S(1)} %copy-done.2), channel_id=1, replica_groups=mesh['gx'=24,'gy'=32] {'gx'}, dimensions={0}, use_global_device_ids=true | all-gather | bytes 614400 | tf_op jit(solution)/shard_map/all_gather | solution.py:23
  453.9 2.4 fusion
  456.3 1.2 copy.8
  457.5 6.3 %all-gather.5.cloned.1.call-done = bf16[768,1024]{1,0:T(8,128)(2,1)} async-done(((bf16[24,1024]{1,0:T(8,128)(2,1)}), bf16[768,1024]{1,0:T(8,128)(2,1)}) %all-gather.5.cloned.1.call-update) | async-done | bytes 1572880 | tf_op jit(solution)/shard_map/all_gather | solution.py:37
  463.8 3.3 convolution_convert_fusion
  467.1 157.5 %reduce-scatter.5.cloned.1.call-done = f32[32,384]{1,0:T(8,128)} async-done(((f32[768,384]{1,0:T(8,128)}), f32[32,384]{1,0:T(8,128)}) %reduce-scatter.5.cloned.1.call-update) | async-done | bytes 49168 | tf_op jit(solution)/shard_map/reduce_scatter | solution.py:47
  624.7 1.4 convert_element_type.23
Async XLA Ops:
  7.2 91.4 %copy-start = (bf16[1024,384]{1,0:T(8,128)(2,1)S(1)}, bf16[1024,384]{1,0:T(8,128)(2,1)}, u32[]{:S(2)}) copy-start(bf16[1024,384]{1,0:T(8,128)(2,1)} %param.8) | copy-start | bytes 2359300
  7.2 255.5 %reduce-scatter.3.cloned.1.call-start = ((), (), s32[]{:S(2)}) async-start(), calls=%async_computation.2 | async-start | bytes 3244032 | tf_op jit(solution)/shard_map/reduce_scatter | solution.py:27
  101.2 161.6 %copy-start.1 = (bf16[24,1024]{1,0:T(8,128)(2,1)S(1)}, bf16[24,1024]{1,0:T(8,128)(2,1)}, u32[]{:S(2)}) copy-start(bf16[24,1024]{1,0:T(8,128)(2,1)} %param.6) | copy-start | bytes 147460
  101.2 261.9 %copy-start.3 = (bf16[384,1024]{1,0:T(8,128)(2,1)S(1)}, bf16[384,1024]{1,0:T(8,128)(2,1)}, u32[]{:S(2)}) copy-start(bf16[384,1024]{1,0:T(8,128)(2,1)} %param.7) | copy-start | bytes 2359300
  101.2 261.9 %all-gather.3.cloned.1.call-start = ((), (), s32[]{:S(2)}) async-start(), calls=%async_computation.3 | async-start | bytes 1622016 | tf_op jit(solution)/shard_map/all_gather | solution.py:38
  264.3 199.5 %all-gather.5.cloned.1.call-start = ((), (), s32[]{:S(2)}) async-start(), calls=%async_computation.5 | async-start | bytes 1622016 | tf_op jit(solution)/shard_map/all_gather | solution.py:37
  265.1 101.5 %copy-start.2 = (bf16[32,384]{1,0:T(8,128)(2,1)S(1)}, bf16[32,384]{1,0:T(8,128)(2,1)}, u32[]{:S(2)}) copy-start(bf16[32,384]{1,0:T(8,128)(2,1)} %param.5) | copy-start | bytes 73732
  265.1 359.6 %reduce-scatter.5.cloned.1.call-start = ((), (), s32[]{:S(2)}) async-start(), calls=%async_computation.4 | async-start | bytes 1228800 | tf_op jit(solution)/shard_map/reduce_scatter | solution.py:47
Sparse Core Ops, SparseCore 0:
  101.3 161.3 reduce-scatter.2
  267.2 95.8 all-gather.2
  367.6 96.1 all-gather.4
  466.8 157.8 reduce-scatter.4
where the time goes:
time: 633 us
  waiting for transfers between devices  424 us (67%)
  blocking collectives  179 us (28%)
  between operations  13.8 us (2%)
  matrix products  11.8 us (2%)
    reduce_scatter x1, waiting for transfers between devices, per_device(): lax.psum_scatter(lax.dot_general(portion, w_out, (((1,), (1,)), ((), ()))...  161 us
    reduce_scatter x1, waiting for transfers between devices, per_device(): lax.psum_scatter(lax.dot_general(portion, w_in, (((1,), (1,)), ((), ())),...  158 us
    all_gather x1, waiting for transfers between devices, per_device(): lax.all_gather(hidden_grad_rows, 'gy', axis=0, tiled=True)  98 us
    all_gather x1, blocking collectives, per_device(): lax.all_gather(out_grad, 'gx', axis=0, tiled=True)  91.3 us
    all_gather x1, blocking collectives, per_device(): lax.all_gather(inputs, 'gx', axis=0, tiled=True)  87.3 us
  transfers between devices with their start and end apart: 4, of which 4 were waited for; matrix products, arithmetic and copies ran while one was open for 2% of the time, Pallas kernels for 0%

commit v1 on v0

v1 whole, which is shorter than its diff:
```python
import functools

import jax
import jax.numpy as jnp
from jax import lax
from jax.experimental import pallas as pl
from jax.experimental.pallas import tpu as pltpu
from jax.sharding import PartitionSpec as P

gelu_scale = 0.7978845608028654
cubic_coef = 0.044715
MESH = pl.DeviceIdType.MESH
NX = 4
K = 2
bf16, f32 = jnp.bfloat16, jnp.float32


def activation(values):
    argument = gelu_scale * (values + cubic_coef * values * values * values)
    tangent = jnp.tanh(argument)
    acts = (0.5 * values * (1.0 + tangent)).astype(bf16)
    slope = 0.5 * (1.0 + tangent) + 0.5 * values * (1.0 - tangent * tangent) * gelu_scale * (
        1.0 + 3.0 * cubic_coef * values * values
    )
    return acts, slope


def dot_nt(a, b):
    return lax.dot_general(a, b, (((1,), (1,)), ((), ())), preferred_element_type=f32)


def dot_tn(a, b):
    return lax.dot_general(a, b, (((0,), (0,)), ((), ())), preferred_element_type=f32)


class Counter:
    def __init__(self):
        self.n = 0

    def take(self, n=1):
        base = self.n
        self.n += n
        return base


def layout(NZ, NY):
    c, r = Counter(), {}
    for name, n in (
        ("og_z", NZ), ("og_x", 6), ("og_c", 2 * NX), ("in_z", NZ), ("in_x", 6),
        ("wo", 1), ("pre_c", 1), ("pre_z", 1),
        ("act_l", 2 * (NY // 2)), ("act_s", 2 * (NY // 2)), ("act_c", 2 * NY),
        ("rs_l", K * (NY // 2)), ("rs_s", K * (NY // 2)), ("zx", K),
        ("gh_l", K * (NY // 2)), ("gh_s", K * (NY // 2)), ("gh_c", K * NY),
        ("xs", 3 * (2 * NY // NX)), ("zs", NZ),
    ):
        r[name] = c.take(n)
    return r, c.n


def count_sends(NZ, NY):
    return 2 * ((NZ - 1) + 6) + 2 * NX + 3 + 2 * (NY - 1 + NY) + K * (NY - 1) + K + K * (2 * NY - 1) + 2 * NY + NZ - 1


def kernel(
    NZ, NY, in_ref, pre_ref, wi_hbm, wo_hbm, og_ref,
    gi_ref, gwi_hbm, gwo_hbm,
    og, ogo, inp, wi, wo, wo_oth, pre_s, pre_r, prez_s, prez_r, slope, acts, part,
    rl_s, rl_r, rs_s, rs_r, tot, zx_s, zx_r, gh, xs_s, xs_r, xs_own, z_own, z_s, z_r, gwi, gwo,
    send, recv, local,
):
    NZg = NZ // 2
    R, W = og_ref.shape
    H = wo_hbm.shape[0]
    Hh, HC = H // 2, H // 2 // K
    T = R * NX * NZ
    XR = R * NZ
    B = T // (2 * NY)
    TB = B // 2
    LL, LS = NY // 2, NY // 2 - 1
    BX = 2 * NY // NX
    S, _ = layout(NZ, NY)

    gx, gy = lax.axis_index("gx"), lax.axis_index("gy")
    x, zl = gx // NZ, gx % NZ
    zh, y, c = gy // (2 * NY), (gy // 2) % NY, gy % 2
    oc = 1 - c
    sg = 1 - 2 * c

    def dev(x=x, zl=zl, zh=zh, y=y, c=c):
        return (x * NZ + zl, (zh * NY + y) * 2 + c)

    def ym(v):
        return lax.rem(v + 2 * NY, NY)

    def xm(v):
        return lax.rem(v + 2 * NX, NX)

    core, zpar = dev(c=oc), dev(zh=1 - zh)
    xr, xl, xo = dev(x=xm(x + 1)), dev(x=xm(x - 1)), dev(x=xm(x + 2))
    zoff = sorted(range(1, NZ), key=lambda o: min(o, NZ - o))
    zpeer = {o: lax.rem(zl + o, NZ) for o in zoff}

    sends = []

    def rcopy(src, dst, ri, to, when=None):
        cp = pltpu.make_async_remote_copy(src, dst, send.at[len(sends)], recv.at[ri], device_id=to, device_id_type=MESH)
        sends.append((cp, when))
        if when is None:
            cp.start()
        else:
            pl.when(when)(cp.start)

    def arrived(dst, ri):
        pltpu.make_async_remote_copy(dst, dst, send.at[0], recv.at[ri], device_id=core, device_id_type=MESH).wait_recv()

    lwo = pltpu.make_async_copy(wo_hbm, wo, local.at[0])
    lwi = pltpu.make_async_copy(wi_hbm, wi, local.at[1])
    lwo.start()
    lwi.start()

    partners = [core, zpar, xr, xl, xo, dev(y=ym(y + 1)), dev(y=ym(y - 1))] + [dev(zl=zpeer[o]) for o in zoff]
    barrier = pltpu.get_barrier_semaphore()
    for p in partners:
        pl.semaphore_signal(barrier, inc=1, device_id=p, device_id_type=MESH)

    mine = pl.ds(pl.multiple_of(gx * R, R), R)
    og[mine, :] = og_ref[...]
    inp[mine, :] = in_ref[...]
    pv = pre_ref[...].astype(f32)
    for h in range(2):
        pre_s[h] = pv[:, h * Hh:(h + 1) * Hh]
    pl.semaphore_wait(barrier, len(partners))

    for o in zoff:
        rcopy(og.at[mine, :], og.at[mine, :], S["og_z"] + zl, dev(zl=zpeer[o]))
    rcopy(pre_s.at[oc], pre_r, S["pre_c"], core)
    lwo.wait()
    rcopy(wo.at[pl.ds(pl.multiple_of(oc * Hh, Hh), Hh), :], wo_oth, S["wo"], core)

    def ring_first(view, sl, ss, sc, sgn):
        rcopy(view(y), view(y), sl, dev(y=ym(y + sgn)))
        if LS:
            rcopy(view(y), view(y), ss, dev(y=ym(y - sgn)))
        rcopy(view(y), view(y), sc + y, core)

    def ring_step(view, sl, ss, sc, sgn, s):
        a, b = ym(y - sgn * s), ym(y + sgn * s)
        arrived(view(a), sl + s - 1)
        if s < LL:
            rcopy(view(a), view(a), sl + s, dev(y=ym(y + sgn)))
        rcopy(view(a), view(a), sc + a, core)
        if s <= LS:
            arrived(view(b), ss + s - 1)
            if s < LS:
                rcopy(view(b), view(b), ss + s, dev(y=ym(y - sgn)))
            rcopy(view(b), view(b), sc + b, core)

    def act_view(q):
        return lambda o: acts.at[c, q, o]

    def act_first(i):
        q = zh if i == 0 else 1 - zh
        ring_first(act_view(q), S["act_l"] + i * LL, S["act_s"] + i * LL, S["act_c"] + i * NY, sg * (1 - 2 * i))

    def act_step(i, s):
        q = zh if i == 0 else 1 - zh
        ring_step(act_view(q), S["act_l"] + i * LL, S["act_s"] + i * LL, S["act_c"] + i * NY, sg * (1 - 2 * i), s)

    arrived(pre_r, S["pre_c"])
    own, oth = pre_s[c], pre_r[...]
    first = jnp.where(c == 0, own, oth)
    second = jnp.where(c == 0, oth, own)
    block = jnp.concatenate([first, second], axis=0)
    prez_s[...] = block.astype(bf16)
    rcopy(prez_s, prez_r, S["pre_z"], zpar)
    a, d = activation(block)
    acts[c, zh, y] = a
    slope[zh] = d
    act_first(0)

    def rows(xi, g):
        return pl.ds(pl.multiple_of(xi * XR + g * NZg * R, NZg * R), NZg * R)

    def z_arrived(buf, base, g):
        for t in range(g * NZg, (g + 1) * NZg):
            def go(t=t):
                there = pl.ds(pl.multiple_of((x * NZ + t) * R, R), R)
                arrived(buf.at[there, :], base + t)
            pl.when(zl != t)(go)

    def to_core(xi, g):
        v = rows(xi, g)
        rcopy(og.at[v, :], ogo.at[v, :], S["og_c"] + xi * 2 + g, core)

    def x_first(buf, zbase, xbase, g):
        z_arrived(buf, zbase, g)
        v = buf.at[rows(x, g), :]
        rcopy(v, v, xbase + g, xr)
        rcopy(v, v, xbase + 2 + g, xl)

    left, right, opp = xm(x - 1), xm(x + 1), xm(x + 2)

    def x_left(buf, xbase, g):
        v = buf.at[rows(left, g), :]
        arrived(v, xbase + g)
        if g == 0:
            rcopy(v, v, xbase + 4, xr)

    def x_right(buf, xbase, g):
        v = buf.at[rows(right, g), :]
        arrived(v, xbase + 2 + g)
        if g == 1:
            rcopy(v, v, xbase + 5, xl)

    def x_opp(buf, xbase, g):
        arrived(buf.at[rows(opp, g), :], xbase + 4 + g)

    for g in range(2):
        x_first(og, S["og_z"], S["og_x"], g)
        to_core(x, g)
    act_step(0, 1)
    x_left(og, S["og_x"], 0)
    x_right(og, S["og_x"], 1)
    to_core(left, 0)
    to_core(right, 1)
    x_left(og, S["og_x"], 1)
    to_core(left, 1)
    x_right(og, S["og_x"], 0)
    to_core(right, 0)
    for o in zoff:
        rcopy(inp.at[mine, :], inp.at[mine, :], S["in_z"] + zl, dev(zl=zpeer[o]))

    arrived(prez_r, S["pre_z"])
    a, d = activation(prez_r[...].astype(f32))
    acts[c, 1 - zh, y] = a
    slope[1 - zh] = d
    act_first(1)
    if LL >= 2:
        act_step(0, 2)
    for g in range(2):
        x_opp(og, S["og_x"], g)
        to_core(opp, g)
    arrived(wo_oth, S["wo"])
    for xi in range(NX):
        for g in range(2):
            arrived(ogo.at[rows(xi, g), :], S["og_c"] + xi * 2 + g)

    w_mine = wo.at[pl.ds(pl.multiple_of(c * Hh, Hh), Hh), :]

    def grad_act(dests):
        def lhs(buf):
            return jnp.concatenate(
                [buf[pl.ds(pl.multiple_of((q * NY + d) * B, B), B), :] for d in dests for q in range(2)], axis=0
            )

        v = dot_nt(lhs(og), w_mine[...]) + dot_nt(lhs(ogo), wo_oth[...])
        for i, d in enumerate(dests):
            for q in range(2):
                r0 = (2 * i + q) * B
                for k in range(K):
                    part[k, q, d] = v[r0:r0 + B, k * HC:(k + 1) * HC]

    sk = [sg, -sg]

    def rs_long(k, s):
        d = ym(y + sk[k] * (LL - s + 1))
        v = part[k, :, d]
        if s > 1:
            arrived(rl_r.at[k, s - 2], S["rs_l"] + k * LL + s - 2)
            v = v + rl_r[k, s - 2].astype(f32)
        rl_s[k, s - 1] = v.astype(bf16)
        rcopy(rl_s.at[k, s - 1], rl_r.at[k, s - 1], S["rs_l"] + k * LL + s - 1, dev(y=ym(y + sk[k])))

    def rs_short(k, s):
        d = ym(y - sk[k] * (LS - s + 1))
        v = part[k, :, d]
        if s > 1:
            arrived(rs_r.at[k, s - 2], S["rs_s"] + k * LL + s - 2)
            v = v + rs_r[k, s - 2].astype(f32)
        rs_s[k, s - 1] = v.astype(bf16)
        rcopy(rs_s.at[k, s - 1], rs_r.at[k, s - 1], S["rs_s"] + k * LL + s - 1, dev(y=ym(y - sk[k])))

    grad_act([ym(y + LL)])
    for k in range(K):
        rs_long(k, 1)
    for dist in range(LL - 1, 0, -1):
        grad_act([ym(y + dist), ym(y - dist)])
        if dist == LL - 1:
            for k in range(K):
                rs_short(k, 1)
    grad_act([y])

    for s in range(2, LL + 1):
        for k in range(K):
            rs_long(k, s)
        if s <= LS:
            for k in range(K):
                rs_short(k, s)
        if s == 2:
            for g in range(2):
                x_first(inp, S["in_z"], S["in_x"], g)
            act_step(1, 1)
            if LL >= 3:
                act_step(0, 3)
        if s == 3:
            for g in range(2):
                x_left(inp, S["in_x"], g)
                x_right(inp, S["in_x"], g)
            if LL >= 4:
                act_step(0, 4)
            act_step(1, 2)

    for k in range(K):
        v = part[k, :, y]
        arrived(rl_r.at[k, LL - 1], S["rs_l"] + k * LL + LL - 1)
        v = v + rl_r[k, LL - 1].astype(f32)
        if LS:
            arrived(rs_r.at[k, LS - 1], S["rs_s"] + k * LL + LS - 1)
            v = v + rs_r[k, LS - 1].astype(f32)
        tot[k] = v
        zx_s[k] = v.astype(bf16)
        rcopy(zx_s.at[k], zx_r.at[k], S["zx"] + k, zpar)

    if LL < 3:
        for g in range(2):
            x_left(inp, S["in_x"], g)
            x_right(inp, S["in_x"], g)
        act_step(1, 2)
    for s in range(3, LL + 1):
        act_step(1, s)
    for g in range(2):
        x_opp(inp, S["in_x"], g)

    def gh_view(k):
        return lambda o: gh.at[c, k, :, o]

    for k in range(K):
        arrived(zx_r.at[k], S["zx"] + k)
        v = tot[k] + zx_r[k].astype(f32)
        gh[c, k, :, y] = (v * slope[:, :, k * HC:(k + 1) * HC]).astype(bf16)
        ring_first(gh_view(k), S["gh_l"] + k * LL, S["gh_s"] + k * LL, S["gh_c"] + k * NY, sk[k])

    for i in range(2):
        q = zh if i == 0 else 1 - zh
        for o in range(NY):
            arrived(acts.at[oc, q, o], S["act_c"] + i * NY + o)
    lgo = []

    def grad_w_out(h, k):
        lhs = acts[h].reshape(T, Hh)[:, k * HC:(k + 1) * HC]
        r = slice(h * Hh + k * HC, h * Hh + (k + 1) * HC)
        gwo[r, :] = dot_tn(lhs, og[...]).astype(bf16)
        cp = pltpu.make_async_copy(gwo.at[r, :], gwo_hbm.at[r, :], local.at[2 + h * K + k])
        cp.start()
        lgo.append(cp)

    pieces = [(h, k) for h in range(2) for k in range(K)]

    def grad_in(dests):
        for o in dests:
            for k in range(K):
                arrived(gh.at[oc, k, :, o], S["gh_c"] + k * NY + o)
        v = None
        for h, k in pieces:
            lhs = jnp.concatenate([gh[h, k, :, o].reshape(2 * B, HC) for o in dests], axis=0)
            u = dot_nt(lhs, wi[:, h * Hh + k * HC:h * Hh + (k + 1) * HC])
            v = u if v is None else v + u
        for i, o in enumerate(dests):
            for q in range(2):
                val = v[(2 * i + q) * B:(2 * i + q + 1) * B]
                number = q * NY + o
                owner, j = number // BX, lax.rem(number, BX)
                rel = xm(owner - x)
                xs_s[q, o] = val.astype(bf16)

                def keep(val=val, j=j):
                    xs_own[j] = val

                pl.when(rel == 0)(keep)
                slot = lax.rem(rel + 2, 3)
                rcopy(xs_s.at[q, o], xs_r.at[slot, j], S["xs"] + slot * BX + j, dev(x=owner), when=rel != 0)

    grad_w_out(*pieces[0])
    lwi.wait()
    queue = [[y]] + [[ym(y + s), ym(y - s)] for s in range(1, LL)] + [[ym(y + LL)]]
    for s in range(1, LL + 1):
        for k in range(K):
            ring_step(gh_view(k), S["gh_l"] + k * LL, S["gh_s"] + k * LL, S["gh_c"] + k * NY, sk[k], s)
        grad_in(queue[s - 1])
        if s < len(pieces):
            grad_w_out(*pieces[s])
    grad_in(queue[LL])
    for p in pieces[LL + 1 if LL < len(pieces) else len(pieces):]:
        grad_w_out(*p)

    def grad_w_in(h, k):
        rhs = gh[h, k].reshape(T, HC)
        r = slice(h * Hh + k * HC, h * Hh + (k + 1) * HC)
        gwi[:, r] = dot_tn(inp[...], rhs).astype(bf16)
        cp = pltpu.make_async_copy(gwi.at[:, r], gwi_hbm.at[:, r], local.at[2 + 2 * K + h * K + k])
        cp.start()
        lgo.append(cp)

    for p in pieces[:2]:
        grad_w_in(*p)

    for j in range(BX):
        v = xs_own[j]
        for slot in range(3):
            arrived(xs_r.at[slot, j], S["xs"] + slot * BX + j)
            v = v + xs_r[slot, j].astype(f32)
        z_own[j * B:(j + 1) * B, :] = v
        z_s[j * B:(j + 1) * B, :] = v.astype(bf16)
    for o in reversed(zoff):
        v = z_s.at[pl.ds(pl.multiple_of(zpeer[o] * R, R), R), :]
        rcopy(v, z_r.at[zl], S["zs"] + zl, dev(zl=zpeer[o]))
    for p in pieces[2:]:
        grad_w_in(*p)
    v = z_own[pl.ds(pl.multiple_of(zl * R, R), R), :]
    for o in zoff:
        arrived(z_r.at[zpeer[o]], S["zs"] + zpeer[o])
        v = v + z_r[zpeer[o]].astype(f32)
    gi_ref[...] = v.astype(bf16)

    for cp, when in sends:
        if when is None:
            cp.wait_send()
        else:
            pl.when(when)(cp.wait_send)
    for cp in lgo:
        cp.wait()


def per_device(n_gx, n_gy, inputs, preact, w_in, w_out, out_grad):
    NZ, NY = n_gx // NX, n_gy // 4
    R, W = out_grad.shape
    H = w_out.shape[0]
    Hh, HC = H // 2, H // 2 // K
    T = R * n_gx
    B = T // (2 * NY)
    BX = 2 * NY // NX
    LL = NY // 2
    _, n_recv = layout(NZ, NY)
    V = pltpu.VMEM
    flops = 8 * T * W * H
    return pl.pallas_call(
        functools.partial(kernel, NZ, NY),
        out_shape=(
            jax.ShapeDtypeStruct((R, W), bf16),
            jax.ShapeDtypeStruct((W, H), bf16),
            jax.ShapeDtypeStruct((H, W), bf16),
        ),
        in_specs=[
            pl.BlockSpec(memory_space=V), pl.BlockSpec(memory_space=V),
            pl.BlockSpec(memory_space=pl.ANY), pl.BlockSpec(memory_space=pl.ANY),
            pl.BlockSpec(memory_space=V),
        ],
        out_specs=(
            pl.BlockSpec(memory_space=V), pl.BlockSpec(memory_space=pl.ANY), pl.BlockSpec(memory_space=pl.ANY),
        ),
        scratch_shapes=[
            V((T, W), bf16), V((T, W), bf16), V((T, W), bf16),
            V((W, H), bf16), V((H, W), bf16), V((Hh, W), bf16),
            V((2, B // 2, Hh), f32), V((B // 2, Hh), f32), V((B, Hh), bf16), V((B, Hh), bf16),
            V((2, B, Hh), f32), V((2, 2, NY, B, Hh), bf16), V((K, 2, NY, B, HC), f32),
            V((K, LL, 2, B, HC), bf16), V((K, LL, 2, B, HC), bf16),
            V((K, LL, 2, B, HC), bf16), V((K, LL, 2, B, HC), bf16),
            V((K, 2, B, HC), f32), V((K, 2, B, HC), bf16), V((K, 2, B, HC), bf16),
            V((2, K, 2, NY, B, HC), bf16),
            V((2, NY, B, W), bf16), V((3, BX, B, W), bf16), V((BX, B, W), f32),
            V((R * NZ, W), f32), V((R * NZ, W), bf16), V((NZ, R, W), bf16),
            V((W, H), bf16), V((H, W), bf16),
            pltpu.SemaphoreType.DMA((count_sends(NZ, NY),)),
            pltpu.SemaphoreType.DMA((n_recv,)),
            pltpu.SemaphoreType.DMA((2 + 4 * K,)),
        ],
        compiler_params=pltpu.CompilerParams(
            collective_id=0, has_side_effects=True, vmem_limit_bytes=40 * 1024 * 1024
        ),
        cost_estimate=pl.CostEstimate(flops=flops, bytes_accessed=8 * W * H, transcendentals=2 * B * Hh),
    )(inputs, preact, w_in, w_out, out_grad)


def solution(mesh):
    n_gx, n_gy = mesh.shape["gx"], mesh.shape["gy"]
    placed = (P("gx", "gy"), P("gy", "gx"), P("gy", "gx"), P("gx", "gy"), P("gx", "gy"))
    return jax.shard_map(
        functools.partial(per_device, n_gx, n_gy),
        mesh=mesh,
        in_specs=placed,
        out_specs=(P("gx", "gy"), P("gy", "gx"), P("gx", "gy")),
        check_vma=False,
    )
```

time: 633 us -> 97.5 us (0.15)
  the two profiles are of different devices: /device:TPU:8 before, /device:TPU:6 now
where the time goes in v1:
time: 97.5 us; the launch traced here: 96.8 us
  Pallas kernels  89.3 us (92%)
  local copies, waits for them, and re-layouts  6.9 us (7%)
    pallas_call x1, Pallas kernels, per_device(): pl.pallas_call(functools.partial(kernel, NZ, NY), out_shape=(jax.ShapeDty...  89.3 us
    unnamed x13, local copies, waits for them, and re-layouts  6.9 us

profile of v1, /device:TPU:6, one launch (start us, length us, event | category | flops | bytes accessed | tf_op | source)
XLA Modules:
  0.0 96.8 jit_solution(9841215688025662234)
XLA Ops:
  0.6 0.0 copy-start
  0.6 1.1 %copy-done = bf16[384,1024]{1,0:T(8,128)(2,1)S(1)} copy-done((bf16[384,1024]{1,0:T(8,128)(2,1)S(1)}, bf16[384,1024]{1,0:T(8,128)(2,1)}, u32[]{:S(2)}) %copy-start) | copy-done | bytes 786456
  1.8 0.0 copy-start.1
  1.8 1.1 %copy-done.1 = bf16[1024,384]{1,0:T(8,128)(2,1)S(1)} copy-done((bf16[1024,384]{1,0:T(8,128)(2,1)S(1)}, bf16[1024,384]{1,0:T(8,128)(2,1)}, u32[]{:S(2)}) %copy-start.1) | copy-done | bytes 786456
  2.9 0.0 copy-start.2
  2.9 0.8 copy-done.2
  3.7 0.0 copy-start.3
  3.7 0.7 copy-done.3
  4.4 0.0 copy-start.4
  4.4 0.7 copy-done.4
  5.2 89.3 %shard_map.76 = (bf16[32,384]{1,0:T(8,128)(2,1)S(1)}, bf16[384,1024]{1,0:T(8,128)(2,1)S(1)}, bf16[1024,384]{1,0:T(8,128)(2,1)S(1)}) custom-call(bf16[32,384]{1,0:T(8,128)(2,1)S(1)} %copy-done.3, bf16[24,1024]{1,0:T(8,128)(2,1)S(1)} %copy-done.2, bf16[384,1024]{1,0:T(8,128)(2,1)S(1)} %copy-done, bf16[1024,384]{1,0:T(8,128)(2,1)S(1)} %copy-done.1, ...), custom_call_target="tpu_custom_call" | custom-call | flops 2415919104 | bytes 3145728 | tf_op jit(solution)/shard_map/pallas_call | solution.py:446
  94.4 0.6 copy.11
  95.1 0.9 copy.12
  95.9 0.9 copy.13
Async XLA Ops:
  0.6 1.1 %copy-start = (bf16[384,1024]{1,0:T(8,128)(2,1)S(1)}, bf16[384,1024]{1,0:T(8,128)(2,1)}, u32[]{:S(2)}) copy-start(bf16[384,1024]{1,0:T(8,128)(2,1)} %wi_hbm.1) | copy-start | bytes 2359300
  1.8 1.1 %copy-start.1 = (bf16[1024,384]{1,0:T(8,128)(2,1)S(1)}, bf16[1024,384]{1,0:T(8,128)(2,1)}, u32[]{:S(2)}) copy-start(bf16[1024,384]{1,0:T(8,128)(2,1)} %wo_hbm.1) | copy-start | bytes 2359300
  2.9 0.8 copy-start.2
  3.7 0.7 copy-start.3
  4.4 0.7 copy-start.4

commit v2 on v1

v2 whole, which is shorter than its diff:
```python
import functools

import jax
import jax.numpy as jnp
from jax import lax
from jax.experimental import pallas as pl
from jax.experimental.pallas import tpu as pltpu
from jax.sharding import PartitionSpec as P

gelu_scale = 0.7978845608028654
cubic_coef = 0.044715
MESH = pl.DeviceIdType.MESH
NX = 4
K = 4
U = 16
bf16, f32 = jnp.bfloat16, jnp.float32


def activation(values):
    argument = gelu_scale * (values + cubic_coef * values * values * values)
    tangent = jnp.tanh(argument)
    acts = (0.5 * values * (1.0 + tangent)).astype(bf16)
    slope = 0.5 * (1.0 + tangent) + 0.5 * values * (1.0 - tangent * tangent) * gelu_scale * (
        1.0 + 3.0 * cubic_coef * values * values
    )
    return acts, slope


def dot_nt(a, b):
    return lax.dot_general(a, b, (((1,), (1,)), ((), ())), preferred_element_type=f32)


def dot_tn(a, b):
    return lax.dot_general(a, b, (((0,), (0,)), ((), ())), preferred_element_type=f32)


class Counter:
    def __init__(self):
        self.n = 0

    def take(self, n=1):
        base = self.n
        self.n += n
        return base


def layout(NZ, NY, rows):
    c, r = Counter(), {}
    for name, n in (
        ("og_z", NZ), ("og_x", 3 * NZ), ("og_c", NX), ("in_z", NZ), ("in_x", 3),
        ("wo", 1), ("pre_c", 1), ("pre_z", 1),
        ("act_l", 2 * (NY // 2)), ("act_s", 2 * (NY // 2)), ("act_c", 2 * NY),
        ("rs_l", K * (NY // 2)), ("rs_s", K * (NY // 2)), ("zx", K),
        ("gh_l", K * (NY // 2)), ("gh_s", K * (NY // 2)), ("gh_c", K * NY),
        ("xs", 3 * (2 * NY // NX)), ("zs", NZ * rows // U),
    ):
        r[name] = c.take(n)
    return r, c.n


def count_sends(NZ, NY):
    return 2 * (NZ - 1) + 3 * NZ + NX + 3 + 3 + 2 * (NY - 1 + NY) + K * (NY - 1) + K + K * (2 * NY - 1) + 2 * NY


def kernel(
    NZ, NY, in_hbm, pre_hbm, wi_hbm, wo_hbm, og_hbm,
    gi_ref, gwi_hbm, gwo_hbm,
    pre_v, og, ogo, inp, wi, wo, wo_oth, pre_s, pre_r, prez_s, prez_r, slope, acts, part,
    rl_s, rl_r, rs_s, rs_r, tot, zx_s, zx_r, gh, xs_s, xs_r, xs_own, z_own, z_s, z_r, gwi, gwo,
    send, recv, local,
):
    R, W = og_hbm.shape
    H = wo_hbm.shape[0]
    Hh, HC = H // 2, H // 2 // K
    T = R * NX * NZ
    XR = R * NZ
    B = T // (2 * NY)
    TB = B // 2
    LL, LS = NY // 2, NY // 2 - 1
    BX = 2 * NY // NX
    S, _ = layout(NZ, NY, R)

    gx, gy = lax.axis_index("gx"), lax.axis_index("gy")
    x, zl = gx // NZ, gx % NZ
    zh, y, c = gy // (2 * NY), (gy // 2) % NY, gy % 2
    oc = 1 - c
    sg = 1 - 2 * c

    def dev(x=x, zl=zl, zh=zh, y=y, c=c):
        return (x * NZ + zl, (zh * NY + y) * 2 + c)

    def ym(v):
        return lax.rem(v + 2 * NY, NY)

    def xm(v):
        return lax.rem(v + 2 * NX, NX)

    core, zpar = dev(c=oc), dev(zh=1 - zh)
    xr, xl, xo = dev(x=xm(x + 1)), dev(x=xm(x - 1)), dev(x=xm(x + 2))
    zoff = range(1, NZ)
    zpeer = {o: lax.rem(zl + o, NZ) for o in zoff}
    near = []
    for i in range(NZ - 1):
        t = 0
        for place in range(NZ):
            order = sorted((p for p in range(NZ) if p != place), key=lambda p: abs(p - place))
            t = jnp.where(zl == place, order[i], t)
        near.append(t)

    sends = []

    def rcopy(src, dst, ri, to, when=None):
        cp = pltpu.make_async_remote_copy(src, dst, send.at[len(sends)], recv.at[ri], device_id=to, device_id_type=MESH)
        sends.append((cp, when))
        if when is None:
            cp.start()
        else:
            pl.when(when)(cp.start)

    def arrived(dst, ri):
        pltpu.make_async_remote_copy(dst, dst, send.at[0], recv.at[ri], device_id=core, device_id_type=MESH).wait_recv()

    partners = [core, zpar, xr, xl, xo, dev(y=ym(y + 1)), dev(y=ym(y - 1))] + [dev(zl=zpeer[o]) for o in zoff]
    barrier = pltpu.get_barrier_semaphore()
    for p in partners:
        pl.semaphore_signal(barrier, inc=1, device_id=p, device_id_type=MESH)

    def piece(xi, t):
        return pl.ds(pl.multiple_of((xi * NZ + t) * R, R), R)

    def column(xi):
        return pl.ds(pl.multiple_of(xi * XR, XR), XR)

    mine = piece(x, zl)
    lpre = pltpu.make_async_copy(pre_hbm, pre_v, local.at[3])
    log = pltpu.make_async_copy(og_hbm, og.at[mine, :], local.at[2])
    lwo = pltpu.make_async_copy(wo_hbm, wo, local.at[0])
    lin = pltpu.make_async_copy(in_hbm, inp.at[mine, :], local.at[4])
    lwi = pltpu.make_async_copy(wi_hbm, wi, local.at[1])
    for cp in (lpre, log, lwo, lin, lwi):
        cp.start()
    pl.semaphore_wait(barrier, len(partners))

    for t in reversed(near):
        rcopy(og_hbm, og.at[mine, :], S["og_z"] + zl, dev(zl=t))

    def x_sends(src, dst, base, step):
        rcopy(src, dst, base, xr)
        rcopy(src, dst, base + step, xl)
        rcopy(src, dst, base + 2 * step, xo)

    x_sends(og_hbm, og.at[mine, :], S["og_x"] + zl, NZ)
    lpre.wait()
    pv = pre_v[...].astype(f32)
    for h in range(2):
        pre_s[h] = pv[:, h * Hh:(h + 1) * Hh]
    rcopy(pre_s.at[oc], pre_r, S["pre_c"], core)
    lwo.wait()
    rcopy(wo.at[pl.ds(pl.multiple_of(oc * Hh, Hh), Hh), :], wo_oth, S["wo"], core)

    def ring_first(view, sl, ss, sc, sgn):
        rcopy(view(y), view(y), sl, dev(y=ym(y + sgn)))
        if LS:
            rcopy(view(y), view(y), ss, dev(y=ym(y - sgn)))
        rcopy(view(y), view(y), sc + y, core)

    def ring_step(view, sl, ss, sc, sgn, s):
        a, b = ym(y - sgn * s), ym(y + sgn * s)
        arrived(view(a), sl + s - 1)
        if s < LL:
            rcopy(view(a), view(a), sl + s, dev(y=ym(y + sgn)))
        rcopy(view(a), view(a), sc + a, core)
        if s <= LS:
            arrived(view(b), ss + s - 1)
            if s < LS:
                rcopy(view(b), view(b), ss + s, dev(y=ym(y - sgn)))
            rcopy(view(b), view(b), sc + b, core)

    def act_view(q):
        return lambda o: acts.at[c, q, o]

    def act_first(i):
        q = zh if i == 0 else 1 - zh
        ring_first(act_view(q), S["act_l"] + i * LL, S["act_s"] + i * LL, S["act_c"] + i * NY, sg * (1 - 2 * i))

    def act_step(i, s):
        if s > LL:
            return
        q = zh if i == 0 else 1 - zh
        ring_step(act_view(q), S["act_l"] + i * LL, S["act_s"] + i * LL, S["act_c"] + i * NY, sg * (1 - 2 * i), s)

    arrived(pre_r, S["pre_c"])
    own, oth = pre_s[c], pre_r[...]
    first = jnp.where(c == 0, own, oth)
    second = jnp.where(c == 0, oth, own)
    block = jnp.concatenate([first, second], axis=0)
    prez_s[...] = block.astype(bf16)
    rcopy(prez_s, prez_r, S["pre_z"], zpar)
    a, d = activation(block)
    acts[c, zh, y] = a
    slope[zh] = d
    act_first(0)

    def to_core(xi):
        v = column(xi)
        rcopy(og.at[v, :], ogo.at[v, :], S["og_c"] + xi, core)

    for t in near:
        v = og.at[piece(x, t), :]
        arrived(v, S["og_z"] + t)
        x_sends(v, v, S["og_x"] + t, NZ)
    log.wait()
    to_core(x)
    act_step(0, 1)
    arrived(prez_r, S["pre_z"])
    a, d = activation(prez_r[...].astype(f32))
    acts[c, 1 - zh, y] = a
    slope[1 - zh] = d
    act_first(1)
    sources = (xm(x - 1), xm(x + 1), xm(x + 2))

    def in_first():
        lin.wait()
        for t in reversed(near):
            rcopy(inp.at[mine, :], inp.at[mine, :], S["in_z"] + zl, dev(zl=t))

    def in_x():
        for t in near:
            arrived(inp.at[piece(x, t), :], S["in_z"] + t)
        v = inp.at[column(x), :]
        x_sends(v, v, S["in_x"], 1)

    def in_last():
        for i, xi in enumerate(sources):
            arrived(inp.at[column(xi), :], S["in_x"] + i)

    for i, xi in enumerate(sources):
        for t in range(NZ):
            arrived(og.at[piece(xi, t), :], S["og_x"] + i * NZ + t)
        to_core(xi)
    in_first()
    act_step(0, 2)
    act_step(1, 1)
    arrived(wo_oth, S["wo"])
    for xi in range(NX):
        arrived(ogo.at[column(xi), :], S["og_c"] + xi)

    w_mine = wo.at[pl.ds(pl.multiple_of(c * Hh, Hh), Hh), :]

    def grad_act(dests):
        def lhs(buf):
            return jnp.concatenate(
                [buf[pl.ds(pl.multiple_of((q * NY + d) * B, B), B), :] for d in dests for q in range(2)], axis=0
            )

        v = dot_nt(lhs(og), w_mine[...]) + dot_nt(lhs(ogo), wo_oth[...])
        for i, d in enumerate(dests):
            for q in range(2):
                r0 = (2 * i + q) * B
                for k in range(K):
                    part[k, q, d] = v[r0:r0 + B, k * HC:(k + 1) * HC]

    sk = [sg if k % 2 == 0 else -sg for k in range(K)]

    def rs_long(k, s):
        d = ym(y + sk[k] * (LL - s + 1))
        v = part[k, :, d]
        if s > 1:
            arrived(rl_r.at[k, s - 2], S["rs_l"] + k * LL + s - 2)
            v = v + rl_r[k, s - 2].astype(f32)
        rl_s[k, s - 1] = v.astype(bf16)
        rcopy(rl_s.at[k, s - 1], rl_r.at[k, s - 1], S["rs_l"] + k * LL + s - 1, dev(y=ym(y + sk[k])))

    def rs_short(k, s):
        d = ym(y - sk[k] * (LS - s + 1))
        v = part[k, :, d]
        if s > 1:
            arrived(rs_r.at[k, s - 2], S["rs_s"] + k * LL + s - 2)
            v = v + rs_r[k, s - 2].astype(f32)
        rs_s[k, s - 1] = v.astype(bf16)
        rcopy(rs_s.at[k, s - 1], rs_r.at[k, s - 1], S["rs_s"] + k * LL + s - 1, dev(y=ym(y - sk[k])))

    grad_act([ym(y + LL)])
    for k in range(K):
        rs_long(k, 1)
    for s in range(1, LL + 1):
        near_y = LL - s
        grad_act([ym(y + near_y), ym(y - near_y)] if near_y else [y])
        if s <= LS:
            for k in range(K):
                rs_short(k, s)
        if s < LL:
            for k in range(K):
                rs_long(k, s + 1)

    for k in range(K):
        v = part[k, :, y]
        arrived(rl_r.at[k, LL - 1], S["rs_l"] + k * LL + LL - 1)
        v = v + rl_r[k, LL - 1].astype(f32)
        if LS:
            arrived(rs_r.at[k, LS - 1], S["rs_s"] + k * LL + LS - 1)
            v = v + rs_r[k, LS - 1].astype(f32)
        tot[k] = v
        zx_s[k] = v.astype(bf16)
        rcopy(zx_s.at[k], zx_r.at[k], S["zx"] + k, zpar)

    in_x()
    for s in range(2, LL):
        act_step(0, s + 1)
        act_step(1, s)

    def gh_view(k):
        return lambda o: gh.at[c, k, :, o]

    for k in range(K):
        arrived(zx_r.at[k], S["zx"] + k)
        v = tot[k] + zx_r[k].astype(f32)
        gh[c, k, :, y] = (v * slope[:, :, k * HC:(k + 1) * HC]).astype(bf16)
        ring_first(gh_view(k), S["gh_l"] + k * LL, S["gh_s"] + k * LL, S["gh_c"] + k * NY, sk[k])

    act_step(1, LL)
    for i in range(2):
        q = zh if i == 0 else 1 - zh
        for o in range(NY):
            arrived(acts.at[oc, q, o], S["act_c"] + i * NY + o)
    lgo = []
    HP = Hh // 2
    pieces = [(h, p) for h in range(2) for p in range(2)]

    def columns(h, p):
        return slice(h * Hh + p * HP, h * Hh + (p + 1) * HP)

    def grad_w_out(h, p):
        r = columns(h, p)
        lhs = acts[h].reshape(T, Hh)[:, p * HP:(p + 1) * HP]
        gwo[r, :] = dot_tn(lhs, og[...]).astype(bf16)
        cp = pltpu.make_async_copy(gwo.at[r, :], gwo_hbm.at[r, :], local.at[5 + h * 2 + p])
        cp.start()
        lgo.append(cp)

    def grad_in(dests):
        for o in dests:
            for k in range(K):
                arrived(gh.at[oc, k, :, o], S["gh_c"] + k * NY + o)
        lhs = jnp.concatenate(
            [
                jnp.concatenate([gh[h, k, :, o].reshape(2 * B, HC) for h in range(2) for k in range(K)], axis=1)
                for o in dests
            ],
            axis=0,
        )
        v = dot_nt(lhs, wi[...])
        for i, o in enumerate(dests):
            for q in range(2):
                val = v[(2 * i + q) * B:(2 * i + q + 1) * B]
                number = q * NY + o
                owner, j = number // BX, lax.rem(number, BX)
                rel = xm(owner - x)
                xs_s[q, o] = val.astype(bf16)

                def keep(val=val, j=j):
                    xs_own[j] = val

                pl.when(rel == 0)(keep)
                slot = lax.rem(rel + 2, 3)
                rcopy(xs_s.at[q, o], xs_r.at[slot, j], S["xs"] + slot * BX + j, dev(x=owner), when=rel != 0)

    def x_sum(dests):
        for o in dests:
            for q in range(2):
                number = q * NY + o
                j = lax.rem(number, BX)

                def go(j=j):
                    v = xs_own[j]
                    for slot in range(3):
                        arrived(xs_r.at[slot, j], S["xs"] + slot * BX + j)
                        v = v + xs_r[slot, j].astype(f32)
                    r = pl.ds(pl.multiple_of(j * B, B), B)
                    z_own[r, :] = v
                    z_s[r, :] = v.astype(bf16)
                    for i in range(B // U):
                        u = j * (B // U) + i
                        to, part_of = u // (R // U), lax.rem(u, R // U)
                        cp = pltpu.make_async_remote_copy(
                            z_s.at[pl.ds(pl.multiple_of(u * U, U), U), :],
                            z_r.at[zl, pl.ds(pl.multiple_of(part_of * U, U), U), :],
                            send.at[count_sends(NZ, NY) + u], recv.at[S["zs"] + zl * (R // U) + part_of],
                            device_id=dev(zl=to), device_id_type=MESH,
                        )
                        pl.when(to != zl)(cp.start)

                pl.when(number // BX == x)(go)

    grad_w_out(*pieces[0])
    lwi.wait()
    queue = [[y]] + [[ym(y + s), ym(y - s)] for s in range(1, LL)] + [[ym(y + LL)]]
    for s in range(1, LL + 1):
        for k in range(K):
            ring_step(gh_view(k), S["gh_l"] + k * LL, S["gh_s"] + k * LL, S["gh_c"] + k * NY, sk[k], s)
        grad_in(queue[s - 1])
        if s < len(pieces):
            grad_w_out(*pieces[s])
        if s >= 2:
            x_sum(queue[s - 2])
    grad_in(queue[LL])
    for p in pieces[LL + 1:]:
        grad_w_out(*p)
    x_sum(queue[LL - 1])

    def grad_w_in(h, p):
        r = columns(h, p)
        n = K // 2
        rhs = jnp.concatenate([gh[h, k].reshape(T, HC) for k in range(p * n, (p + 1) * n)], axis=1)
        gwi[:, r] = dot_tn(inp[...], rhs).astype(bf16)
        cp = pltpu.make_async_copy(gwi.at[:, r], gwi_hbm.at[:, r], local.at[9 + h * 2 + p])
        cp.start()
        lgo.append(cp)

    in_last()
    for p in pieces[:2]:
        grad_w_in(*p)

    x_sum(queue[LL])
    for p in pieces[2:]:
        grad_w_in(*p)
    v = z_own[pl.ds(pl.multiple_of(zl * R, R), R), :]
    for t in near:
        for i in range(R // U):
            arrived(z_r.at[t, i * U:(i + 1) * U, :], S["zs"] + t * (R // U) + i)
        v = v + z_r[t].astype(f32)
    gi_ref[...] = v.astype(bf16)

    for u in range(NZ * R // U):
        row = z_s.at[u * U:(u + 1) * U, :]
        cp = pltpu.make_async_remote_copy(
            row, row, send.at[count_sends(NZ, NY) + u], recv.at[0], device_id=core, device_id_type=MESH
        )
        pl.when(zl != u // (R // U))(cp.wait_send)
    for cp, when in sends:
        if when is None:
            cp.wait_send()
        else:
            pl.when(when)(cp.wait_send)
    for cp in lgo:
        cp.wait()


def per_device(n_gx, n_gy, inputs, preact, w_in, w_out, out_grad):
    NZ, NY = n_gx // NX, n_gy // 4
    R, W = out_grad.shape
    H = w_out.shape[0]
    Hh, HC = H // 2, H // 2 // K
    T = R * n_gx
    B = T // (2 * NY)
    BX = 2 * NY // NX
    LL = NY // 2
    _, n_recv = layout(NZ, NY, R)
    V = pltpu.VMEM
    flops = 8 * T * W * H
    return pl.pallas_call(
        functools.partial(kernel, NZ, NY),
        out_shape=(
            jax.ShapeDtypeStruct((R, W), bf16),
            jax.ShapeDtypeStruct((W, H), bf16),
            jax.ShapeDtypeStruct((H, W), bf16),
        ),
        in_specs=[
            pl.BlockSpec(memory_space=pltpu.HBM),
        ] * 5,
        out_specs=(
            pl.BlockSpec(memory_space=V), pl.BlockSpec(memory_space=pl.ANY), pl.BlockSpec(memory_space=pl.ANY),
        ),
        scratch_shapes=[
            V((B // 2, H), bf16), V((T, W), bf16), V((T, W), bf16), V((T, W), bf16),
            V((W, H), bf16), V((H, W), bf16), V((Hh, W), bf16),
            V((2, B // 2, Hh), f32), V((B // 2, Hh), f32), V((B, Hh), bf16), V((B, Hh), bf16),
            V((2, B, Hh), f32), V((2, 2, NY, B, Hh), bf16), V((K, 2, NY, B, HC), f32),
            V((K, LL, 2, B, HC), bf16), V((K, LL, 2, B, HC), bf16),
            V((K, LL, 2, B, HC), bf16), V((K, LL, 2, B, HC), bf16),
            V((K, 2, B, HC), f32), V((K, 2, B, HC), bf16), V((K, 2, B, HC), bf16),
            V((2, K, 2, NY, B, HC), bf16),
            V((2, NY, B, W), bf16), V((3, BX, B, W), bf16), V((BX, B, W), f32),
            V((R * NZ, W), f32), V((R * NZ, W), bf16), V((NZ, R, W), bf16),
            V((W, H), bf16), V((H, W), bf16),
            pltpu.SemaphoreType.DMA((count_sends(NZ, NY) + NZ * R // U,)),
            pltpu.SemaphoreType.DMA((n_recv,)),
            pltpu.SemaphoreType.DMA((13,)),
        ],
        compiler_params=pltpu.CompilerParams(
            collective_id=0, has_side_effects=True, vmem_limit_bytes=60 * 1024 * 1024
        ),
        cost_estimate=pl.CostEstimate(flops=flops, bytes_accessed=8 * W * H, transcendentals=2 * B * Hh),
    )(inputs, preact, w_in, w_out, out_grad)


def solution(mesh):
    n_gx, n_gy = mesh.shape["gx"], mesh.shape["gy"]
    placed = (P("gx", "gy"), P("gy", "gx"), P("gy", "gx"), P("gx", "gy"), P("gx", "gy"))
    return jax.shard_map(
        functools.partial(per_device, n_gx, n_gy),
        mesh=mesh,
        in_specs=placed,
        out_specs=(P("gx", "gy"), P("gy", "gx"), P("gx", "gy")),
        check_vma=False,
    )
```

time: 97.5 us -> 88.6 us (0.909)
  Pallas kernels: 89.3 us -> 83.1 us
  local copies, waits for them, and re-layouts: 6.9 us -> 4.37 us
    pallas_call x1, Pallas kernels: 89.3 us -> 83.1 us  [per_device(): pl.pallas_call(functools.partial(kernel, NZ, NY), out_shape=(jax.ShapeDty...]
    unnamed x13 -> x5, local copies, waits for them, and re-layouts: 6.9 us -> 4.37 us
where the time goes in v2:
time: 88.6 us; the launch traced here: 88.1 us
  Pallas kernels  83.1 us (94%)
  local copies, waits for them, and re-layouts  4.37 us (5%)
    pallas_call x1, Pallas kernels, per_device(): pl.pallas_call(functools.partial(kernel, NZ, NY), out_shape=(jax.ShapeDty...  83.1 us
    unnamed x5, local copies, waits for them, and re-layouts  4.37 us

profile of v2, /device:TPU:6, one launch (start us, length us, event | category | flops | bytes accessed | tf_op | source)
XLA Modules:
  0.0 88.1 jit_solution(3763423492984271458)
XLA Ops:
  0.6 83.1 %shard_map.76 = (bf16[32,384]{1,0:T(8,128)(2,1)}, bf16[384,1024]{1,0:T(8,128)(2,1)}, bf16[1024,384]{1,0:T(8,128)(2,1)}) custom-call(bf16[32,384]{1,0:T(8,128)(2,1)} %in_hbm.1, bf16[24,1024]{1,0:T(8,128)(2,1)} %pre_hbm.1, bf16[384,1024]{1,0:T(8,128)(2,1)} %wi_hbm.1, bf16[1024,384]{1,0:T(8,128)(2,1)} %wo_hbm.1, bf16[32,384]{1,0:T(8,128)(2,1)} %og_hbm.1), custom_call_target="tpu_custom_call" | custom-call | flops 2415919104 | bytes 3145728 | tf_op jit(solution)/shard_map/pallas_call | solution.py:461
  83.7 1.3 %copy.11 = bf16[32,384]{1,0:T(8,128)(2,1)} copy(bf16[32,384]{1,0:T(8,128)(2,1)} %get-tuple-element.6) | data formatting | bytes 49152
  85.1 0.0 copy-start
  85.1 2.1 %copy.12 = bf16[384,1024]{1,0:T(8,128)(2,1)} copy(bf16[384,1024]{1,0:T(8,128)(2,1)} %get-tuple-element.7) | data formatting | bytes 1572864
  87.2 0.0 copy-done
  87.2 0.9 copy.13
Async XLA Ops:
  85.1 2.1 %copy-start = (bf16[1024,384]{1,0:T(8,128)(2,1)S(1)}, bf16[1024,384]{1,0:T(8,128)(2,1)}, u32[]{:S(2)}) copy-start(bf16[1024,384]{1,0:T(8,128)(2,1)} %get-tuple-element.8) | copy-start | bytes 2359300

commit v3 on v2

--- a/solution.py
+++ b/solution.py
@@ -47,7 +47,7 @@
 def layout(NZ, NY, rows):
     c, r = Counter(), {}
     for name, n in (
-        ("og_z", NZ), ("og_x", 3 * NZ), ("og_c", NX), ("in_z", NZ), ("in_x", 3),
+        ("og_z", NZ), ("og_x", 3 * NZ), ("og_c", 2 * NX), ("in_z", NZ), ("in_x", 3),
         ("wo", 1), ("pre_c", 1), ("pre_z", 1),
         ("act_l", 2 * (NY // 2)), ("act_s", 2 * (NY // 2)), ("act_c", 2 * NY),
         ("rs_l", K * (NY // 2)), ("rs_s", K * (NY // 2)), ("zx", K),
@@ -59,7 +59,7 @@
 
 
 def count_sends(NZ, NY):
-    return 2 * (NZ - 1) + 3 * NZ + NX + 3 + 3 + 2 * (NY - 1 + NY) + K * (NY - 1) + K + K * (2 * NY - 1) + 2 * NY
+    return 2 * (NZ - 1) + 3 * NZ + 2 * NX + 3 + 3 + 2 * (NY - 1 + NY) + K * (NY - 1) + K + K * (2 * NY - 1) + 2 * NY
 
 
 def kernel(
@@ -201,16 +201,20 @@
     slope[zh] = d
     act_first(0)
 
-    def to_core(xi):
-        v = column(xi)
-        rcopy(og.at[v, :], ogo.at[v, :], S["og_c"] + xi, core)
+    def half(xi, g):
+        return pl.ds(pl.multiple_of(xi * XR + g * (XR // 2), XR // 2), XR // 2)
+
+    def to_core(xi, g):
+        v = half(xi, g)
+        rcopy(og.at[v, :], ogo.at[v, :], S["og_c"] + 2 * xi + g, core)
 
     for t in near:
         v = og.at[piece(x, t), :]
         arrived(v, S["og_z"] + t)
         x_sends(v, v, S["og_x"] + t, NZ)
     log.wait()
-    to_core(x)
+    to_core(x, 0)
+    to_core(x, 1)
     act_step(0, 1)
     arrived(prez_r, S["pre_z"])
     a, d = activation(prez_r[...].astype(f32))
@@ -237,13 +241,15 @@
     for i, xi in enumerate(sources):
         for t in range(NZ):
             arrived(og.at[piece(xi, t), :], S["og_x"] + i * NZ + t)
-        to_core(xi)
+            if (t + 1) % (NZ // 2) == 0:
+                to_core(xi, t // (NZ // 2))
     in_first()
     act_step(0, 2)
     act_step(1, 1)
     arrived(wo_oth, S["wo"])
     for xi in range(NX):
-        arrived(ogo.at[column(xi), :], S["og_c"] + xi)
+        for g in range(2):
+            arrived(ogo.at[half(xi, g), :], S["og_c"] + 2 * xi + g)
 
     w_mine = wo.at[pl.ds(pl.multiple_of(c * Hh, Hh), Hh), :]
 
@@ -292,6 +298,8 @@
         if s < LL:
             for k in range(K):
                 rs_long(k, s + 1)
+        if s == 2:
+            in_x()
 
     for k in range(K):
         v = part[k, :, y]
@@ -304,7 +312,6 @@
         zx_s[k] = v.astype(bf16)
         rcopy(zx_s.at[k], zx_r.at[k], S["zx"] + k, zpar)
 
-    in_x()
     for s in range(2, LL):
         act_step(0, s + 1)
         act_step(1, s)
@@ -401,12 +408,11 @@
         grad_in(queue[s - 1])
         if s < len(pieces):
             grad_w_out(*pieces[s])
-        if s >= 2:
-            x_sum(queue[s - 2])
     grad_in(queue[LL])
     for p in pieces[LL + 1:]:
         grad_w_out(*p)
-    x_sum(queue[LL - 1])
+    for dests in queue[:LL]:
+        x_sum(dests)
 
     def grad_w_in(h, p):
         r = columns(h, p)

time: 88.6 us -> 88.8 us (level)
  no operation moved by 1% of the time
where the time goes in v3:
time: 88.8 us; the launch traced here: 88.6 us
  Pallas kernels  83.6 us (94%)
  local copies, waits for them, and re-layouts  4.37 us (5%)
    pallas_call x1, Pallas kernels, per_device(): pl.pallas_call(functools.partial(kernel, NZ, NY), out_shape=(jax.ShapeDty...  83.6 us
    unnamed x5, local copies, waits for them, and re-layouts  4.37 us

profile of v3, /device:TPU:6, one launch (start us, length us, event | category | flops | bytes accessed | tf_op | source)
XLA Modules:
  0.0 88.6 jit_solution(9371907900814711658)
XLA Ops:
  0.6 83.6 %shard_map.76 = (bf16[32,384]{1,0:T(8,128)(2,1)}, bf16[384,1024]{1,0:T(8,128)(2,1)}, bf16[1024,384]{1,0:T(8,128)(2,1)}) custom-call(bf16[32,384]{1,0:T(8,128)(2,1)} %in_hbm.1, bf16[24,1024]{1,0:T(8,128)(2,1)} %pre_hbm.1, bf16[384,1024]{1,0:T(8,128)(2,1)} %wi_hbm.1, bf16[1024,384]{1,0:T(8,128)(2,1)} %wo_hbm.1, bf16[32,384]{1,0:T(8,128)(2,1)} %og_hbm.1), custom_call_target="tpu_custom_call" | custom-call | flops 2415919104 | bytes 3145728 | tf_op jit(solution)/shard_map/pallas_call | solution.py:467
  84.2 1.3 %copy.11 = bf16[32,384]{1,0:T(8,128)(2,1)} copy(bf16[32,384]{1,0:T(8,128)(2,1)} %get-tuple-element.6) | data formatting | bytes 49152
  85.6 0.0 copy-start
  85.6 2.1 %copy.12 = bf16[384,1024]{1,0:T(8,128)(2,1)} copy(bf16[384,1024]{1,0:T(8,128)(2,1)} %get-tuple-element.7) | data formatting | bytes 1572864
  87.7 0.0 copy-done
  87.7 0.9 copy.13
Async XLA Ops:
  85.6 2.1 %copy-start = (bf16[1024,384]{1,0:T(8,128)(2,1)S(1)}, bf16[1024,384]{1,0:T(8,128)(2,1)}, u32[]{:S(2)}) copy-start(bf16[1024,384]{1,0:T(8,128)(2,1)} %get-tuple-element.8) | copy-start | bytes 2359300
